TPU v7x, 512 devices: a whole 4x8x8 slice. The times are simulated.
512 devices in a mesh: rep: 4 (over z_lo), row: 128 (over y, z_hi, x, core).
Axes of the slice: x: 4, y: 8, z: 8 (z_hi: 2, z_lo: 4; z = z_hi * 4 + z_lo), core: 2. Of those that a mesh axis runs over, the one named last changes fastest.
Arguments:
- features: bfloat16 [65536, 128], P(('rep', 'row')), may hold values from -6 to 6
- node_order: int32 [512, 128], P(('rep', 'row')), may hold values from 0 to 127, each once within a row
- tile_values: bfloat16 [4, 128, 135, 128, 128], P('rep', 'row'), as said below
- tile_row: int32 [4, 128, 135], P('rep', 'row'), may hold values from 0 to 3, as said below
- tile_col: int32 [4, 128, 135], P('rep', 'row'), may hold values from 0 to 127
- tile_count: int32 [4, 128], P('rep', 'row'), may hold values from 1 to 135, as said below
- weight: bfloat16 [128, 256], replicated, may hold values from -0.5 to 0.5
- bias_vec: float32 [256], replicated, may hold values from -3 to 3
- cotangent: bfloat16 [65536, 256], P(('rep', 'row')), may hold values from -6 to 6
Outputs:
- activations: bfloat16 [65536, 256], P(('rep', 'row'))
- feature_grad: float32 [65536, 128], P(('rep', 'row'))
- weight_grad: float32 [128, 256], replicated
- bias_grad: float32 [256], replicated
Inputs may be any that keep to these rules, and one draw needn't show every extreme that they name: Slots 0 to tile_count - 1 of a device hold its tiles, later slots hold arbitrary values; some device uses all 135 slots in every draw. Within a device's used slots the pairs (tile_row, tile_col) are distinct. A is symmetric: the tile at block (g, h) is the transpose of the tile at block (h, g). `tile_values`: tiles at used slots assemble the symmetric matrix A.
All inputs are finite; a program needn't handle non-finite values.
Results may differ from a plain program's by a relative error of at most 0.015.
Values may be sent and summed in bfloat16 or wider, within the bound.
A program may use at most 64 MiB of HBM per device.

v0:
```python
import jax
import jax.numpy as jnp
from jax import lax
from jax.sharding import PartitionSpec as P


def combine_tiles(gathered, tile_values, tile_row, tile_col, tile_count):
    replicas = lax.axis_size("rep")
    slot_len = tile_values.shape[2]
    tile_len = tile_values.shape[3]
    feat_len = gathered.shape[1]
    blocks = gathered.reshape(-1, tile_len, feat_len)
    tile_mats = tile_values.reshape(slot_len, tile_len, tile_len)
    row_slot = tile_row.reshape(slot_len)
    col_slot = tile_col.reshape(slot_len)
    used_count = tile_count.reshape(())
    rep_ids = jnp.arange(replicas, dtype=jnp.int32)
    picked = blocks[col_slot]
    products = jnp.einsum("kab,kbw->kaw", tile_mats, picked, preferred_element_type=jnp.float32)
    in_use = jnp.arange(slot_len, dtype=jnp.int32) < used_count
    chosen = ((row_slot[None, :] == rep_ids[:, None]) & in_use[None, :]).astype(jnp.float32)
    partial_value = jnp.einsum("ik,kaw->iaw", chosen, products)
    return partial_value.reshape(replicas * tile_len, feat_len)


def local(
    features, node_order, tile_values, tile_row, tile_col, tile_count, weight, bias_vec, cotangent
):
    order_row = node_order.reshape(-1)
    permuted = features[order_row]
    gathered = lax.all_gather(permuted, "row", axis=0, tiled=True)
    partial_value = combine_tiles(gathered, tile_values, tile_row, tile_col, tile_count)
    hidden = lax.psum_scatter(partial_value, "rep", scatter_dimension=0, tiled=True).astype(
        jnp.bfloat16
    )
    pre_act = jnp.dot(hidden, weight, preferred_element_type=jnp.float32) + bias_vec
    activations = jax.nn.silu(pre_act).astype(jnp.bfloat16)
    sigmoid_pre = jax.nn.sigmoid(pre_act)
    pre_grad = (
        cotangent.astype(jnp.float32) * sigmoid_pre * (1.0 + pre_act * (1.0 - sigmoid_pre))
    ).astype(jnp.bfloat16)
    weight_term = lax.dot_general(
        hidden, pre_grad, (((0,), (0,)), ((), ())), preferred_element_type=jnp.float32
    )
    bias_term = jnp.sum(pre_grad.astype(jnp.float32), axis=0)
    hidden_grad = lax.dot_general(
        pre_grad, weight, (((1,), (1,)), ((), ())), preferred_element_type=jnp.float32
    ).astype(jnp.bfloat16)
    gathered_grad = lax.all_gather(hidden_grad, "row", axis=0, tiled=True)
    partial_grad = combine_tiles(gathered_grad, tile_values, tile_row, tile_col, tile_count)
    permuted_grad = lax.psum_scatter(partial_grad, "rep", scatter_dimension=0, tiled=True)
    weight_grad, bias_grad = lax.psum((weight_term, bias_term), ("rep", "row"))
    feature_grad = jnp.zeros(permuted_grad.shape, jnp.float32).at[order_row].set(permuted_grad)
    return (activations, feature_grad, weight_grad, bias_grad)


def solution(mesh):
    return jax.shard_map(
        local,
        mesh=mesh,
        in_specs=(
            P(("rep", "row"), None),
            P(("rep", "row"), None),
            P("rep", "row", None, None, None),
            P("rep", "row", None),
            P("rep", "row", None),
            P("rep", "row"),
            P(),
            P(),
            P(("rep", "row"), None),
        ),
        out_specs=(P(("rep", "row"), None), P(("rep", "row"), None), P(), P()),
        check_vma=False,
    )
```

profile of v0, /device:TPU:1, one launch (start us, length us, event | category | flops | bytes accessed | tf_op | source)
XLA Modules:
  0.0 677.9 jit_solution(14745059827495938698)
XLA Ops:
  7.2 0.0 all-gather.6.cloned.1.call-start
  7.2 0.7 fusion.15
  7.9 2.0 gather_fusion
  9.9 0.0 all-gather.6.cloned.1.call-update
  9.9 0.0 reduce-scatter.3.cloned.1.call-start
  10.6 0.7 compare_select_fusion
  11.3 147.5 %all-gather.6.cloned.1.call-done = bf16[16384,128]{1,0:T(8,128)(2,1)} async-done(((bf16[128,128]{1,0:T(8,128)(2,1)}), bf16[16384,128]{1,0:T(8,128)(2,1)}) %all-gather.6.cloned.1.call-update) | async-done | bytes 4194320 | tf_op jit(solution)/shard_map/all_gather | solution.py:31
  158.8 9.7 %gather_fusion.1 = bf16[135,128,128]{2,1,0:T(8,128)(2,1)} fusion(bf16[128,128,128]{2,1,0:T(8,128)(2,1)} %bitcast.36, s32[1024]{0:T(1024)S(1)} %pad_clamp_fusion), kind=kCustom, calls=%fused_computation.1 | custom fusion | bytes 8847900 | tf_op jit(solution)/shard_map/gather | solution.py:18
  168.5 8.9 %fusion.6 = bf16[135,128,128]{2,1,0:T(8,128)(2,1)} fusion(bf16[135,128,128]{2,1,0:T(8,128)(2,1)} %gather_fusion.1, bf16[1,1,135,128,128]{4,3,2,1,0:T(8,128)(2,1)} %param.11), kind=kOutput, calls=%fused_computation.10 | convolution fusion | flops 566231040 | bytes 13271040 | tf_op jit(solution)/shard_map/kab,kbw->kaw/dot_general | solution.py:19
  177.5 6.9 %copy.15 = bf16[135,128,128]{1,0,2:T(8,128)(2,1)} copy(bf16[135,128,128]{2,1,0:T(8,128)(2,1)} %fusion.6) | data formatting | bytes 8847360 | tf_op jit(solution)/shard_map/kab,kbw->kaw/dot_general | solution.py:19
  184.4 3.0 fusion.2
  187.4 0.7 copy.13
  188.1 0.0 reduce-scatter.3.cloned.1.call-update
  188.1 0.0 all-gather.4.cloned.1.call-start
  188.2 19.4 %reduce-scatter.3.cloned.1.call-done = f32[128,128]{1,0:T(8,128)} async-done(((f32[512,128]{1,0:T(8,128)}), f32[128,128]{1,0:T(8,128)}) %reduce-scatter.3.cloned.1.call-update) | async-done | bytes 65552 | tf_op jit(solution)/shard_map/reduce_scatter | solution.py:33
  207.6 1.7 convert_reduce_fusion
  209.3 0.8 convolution_convert_fusion
  210.1 0.0 all-gather.4.cloned.1.call-update
  210.1 0.2 reduce-scatter.5.cloned.1.call-start
  210.3 143.5 %all-gather.4.cloned.1.call-done = bf16[16384,128]{1,0:T(8,128)(2,1)} async-done(((bf16[128,128]{1,0:T(8,128)(2,1)}), bf16[16384,128]{1,0:T(8,128)(2,1)}) %all-gather.4.cloned.1.call-update) | async-done | bytes 4194320 | tf_op jit(solution)/shard_map/all_gather | solution.py:49
  353.8 9.7 %gather_fusion.2 = bf16[135,128,128]{2,1,0:T(8,128)(2,1)} fusion(bf16[128,128,128]{2,1,0:T(8,128)(2,1)} %bitcast.37, s32[1024]{0:T(1024)S(1)} %pad_clamp_fusion), kind=kCustom, calls=%fused_computation.2 | custom fusion | bytes 8847900 | tf_op jit(solution)/shard_map/gather | solution.py:18
  363.5 8.9 %fusion.4 = bf16[135,128,128]{2,1,0:T(8,128)(2,1)} fusion(bf16[135,128,128]{2,1,0:T(8,128)(2,1)} %gather_fusion.2, bf16[1,1,135,128,128]{4,3,2,1,0:T(8,128)(2,1)} %param.11), kind=kOutput, calls=%fused_computation.8 | convolution fusion | flops 566231040 | bytes 13271040 | tf_op jit(solution)/shard_map/kab,kbw->kaw/dot_general | solution.py:19
  372.5 6.9 %copy.16 = bf16[135,128,128]{1,0,2:T(8,128)(2,1)} copy(bf16[135,128,128]{2,1,0:T(8,128)(2,1)} %fusion.4) | data formatting | bytes 8847360 | tf_op jit(solution)/shard_map/kab,kbw->kaw/dot_general | solution.py:19
  379.3 3.0 fusion
  382.4 0.7 copy.14
  383.1 0.0 reduce-scatter.5.cloned.1.call-update
  383.1 0.0 all-reduce.2.cloned.1.call-start
  383.2 0.9 fusion.10
  384.1 97.1 %psum.15 = f32[256]{0:T(256)} all-reduce(f32[256]{0:T(256)S(1)} %get-tuple-element.4), channel_id=1, replica_groups=mesh['rep'=4,'row'=128] {'rep','row'}, use_global_device_ids=true, to_apply=%region_5.6 | all-reduce | flops 256 | bytes 2048 | tf_op jit(solution)/shard_map/psum | solution.py:52
  481.2 1.8 scatter_custom_fusion
  483.0 186.8 %all-reduce.2.cloned.1.call-done = f32[128,256]{1,0:T(8,128)} async-done(((f32[128,256]{1,0:T(8,128)}), f32[128,256]{1,0:T(8,128)}) %all-reduce.2.cloned.1.call-update) | async-done | bytes 131088 | tf_op jit(solution)/shard_map/psum | solution.py:52
  669.8 1.6 copy.19
  (15 shorter events, 0.1 us)
Async XLA Ops:
  7.2 200.4 %copy-start = (bf16[128,256]{1,0:T(8,128)(2,1)S(1)}, bf16[128,256]{1,0:T(8,128)(2,1)}, u32[]{:S(2)}) copy-start(bf16[128,256]{1,0:T(8,128)(2,1)} %param.15) | copy-start | bytes 196612
  7.2 151.6 %all-gather.6.cloned.1.call-start = ((), (), s32[]{:S(2)}) async-start(), calls=%async_computation.6 | async-start | bytes 4227072 | tf_op jit(solution)/shard_map/all_gather | solution.py:31
  9.9 197.7 %reduce-scatter.3.cloned.1.call-start = ((), (), s32[]{:S(2)}) async-start(), calls=%async_computation.2 | async-start | bytes 327680 | tf_op jit(solution)/shard_map/reduce_scatter | solution.py:33
  177.5 6.9 %copy-start.2 = (s32[1,1,135]{2,1,0:T(1,128)S(1)}, s32[1,1,135]{2,1,0:T(1,128)}, u32[]{:S(2)}) copy-start(s32[1,1,135]{2,1,0:T(1,128)} %param.12) | copy-start | bytes 1624
  184.4 23.3 %copy-start.3 = (bf16[128,256]{1,0:T(8,128)(2,1)S(1)}, bf16[128,256]{1,0:T(8,128)(2,1)}, u32[]{:S(2)}) copy-start(bf16[128,256]{1,0:T(8,128)(2,1)} %param.17) | copy-start | bytes 196612
  184.4 23.3 %copy-start.4 = (f32[256]{0:T(256)S(1)}, f32[256]{0:T(256)}, u32[]{:S(2)}) copy-start(f32[256]{0:T(256)} %param.16) | copy-start | bytes 3076
  188.1 165.7 %all-gather.4.cloned.1.call-start = ((), (), s32[]{:S(2)}) async-start(), calls=%async_computation.3 | async-start | bytes 4227072 | tf_op jit(solution)/shard_map/all_gather | solution.py:49
  210.1 271.1 %reduce-scatter.5.cloned.1.call-start = ((), (), s32[]{:S(2)}) async-start(), calls=%async_computation.4 | async-start | bytes 327680 | tf_op jit(solution)/shard_map/reduce_scatter | solution.py:51
  379.3 3.8 copy-start.1
  383.1 286.7 %all-reduce.2.cloned.1.call-start = ((), (), s32[]{:S(2)}) async-start(), calls=%async_computation.5 | async-start | bytes 262144 | tf_op jit(solution)/shard_map/psum | solution.py:52
Sparse Core Ops, SparseCore 0:
  13.2 145.6 all-gather.5
  188.3 19.2 reduce-scatter.2
  213.6 140.1 all-gather.3
  383.2 19.3 reduce-scatter.4
  408.0 261.7 all-reduce.1
where the time goes:
time: 679 us; the launch traced here: 678 us
  waiting for transfers between devices  497 us (73%)
  blocking collectives  97.1 us (14%)
  local copies, waits for them, and re-layouts  40 us (6%)
  matrix products  27.2 us (4%)
  between operations  14.5 us (2%)
    psum x1, waiting for transfers between devices, local(): weight_grad, bias_grad = lax.psum((weight_term, bias_term), ('rep', 'row'))  187 us
    all_gather x1, waiting for transfers between devices, local(): gathered = lax.all_gather(permuted, 'row', axis=0, tiled=True)  147 us
    all_gather x1, waiting for transfers between devices, local(): gathered_grad = lax.all_gather(hidden_grad, 'row', axis=0, tiled=True)  143 us
    psum x1, blocking collectives, local(): weight_grad, bias_grad = lax.psum((weight_term, bias_term), ('rep', 'row'))  97.1 us
    gather x2, local copies, waits for them, and re-layouts, combine_tiles(): picked = blocks[col_slot]  19.4 us
    reduce_scatter x1, waiting for transfers between devices, local(): lax.psum_scatter(partial_value, 'rep', scatter_dimension=0, tiled=True)  19.4 us
    dot_general x2, matrix products, combine_tiles(): jnp.einsum('kab,kbw->kaw', tile_mats, picked, preferred_element_type=jnp....  17.9 us
    dot_general x2, local copies, waits for them, and re-layouts, combine_tiles(): jnp.einsum('kab,kbw->kaw', tile_mats, picked, preferred_element_type=jnp....  13.8 us
  transfers between devices with their start and end apart: 5, of which 4 were waited for; matrix products, arithmetic and copies ran while one was open for 0% of the time, Pallas kernels for 0%

commit v1 on v0

v1 whole, which is shorter than its diff:
```python
import functools

import jax
import jax.numpy as jnp
from jax import lax
from jax.experimental import pallas as pl
from jax.experimental.pallas import tpu as pltpu
from jax.sharding import PartitionSpec as P

MESH = pl.DeviceIdType.MESH
NX, NY, NZ = 4, 8, 8
T = 128
R1, R2 = 64, 64
SLOTS = 135
DELTAS = (0, -1, 1, -2, 2, -3, 3, 4)
XIS = (0, -1, 1, 2)
GROUPS = ((0, 1), (1, 2), (3, 2), (5, 3))
ROWS = 64 * (R1 + R2)


def row1(ab, d, xi):
    return ((ab * 8 + d) * 4 + xi) * R1


def row2(ab, xi, d):
    return 64 * R1 + ((ab * 4 + xi) * 8 + d) * R2


def sem_x1(ab):
    return ab


SEM_Z = 2


def sem_y1(ab, d):
    return 3 + ab * 7 + d - 1


def sem_y2(ab, d):
    return 17 + ab * 7 + d - 1


def sem_x2(ab, xi, g):
    return 31 + (ab * 3 + xi - 1) * 4 + g


def sem_sib(ab, g):
    return 55 + ab * 4 + g


N_RECV = 63
SEND_Z, SEND_X1, SEND_Y1, SEND_Y2, SEND_X2, SEND_SIB = range(6)


def kernel(
    features, order, tiles_hbm, table, weight, bias, cotangent,
    act_out, fgrad_out, wgrad_out, bgrad_out,
    tiles, G, acc, part, part_in, wp, wp_in, w2, w2_in, w3, w3_in, wq, wfull,
    tile_sem, recv, send, rs_recv, rs_send, ar_recv, ar_send,
):
    q = lax.axis_index("rep")
    r = lax.axis_index("row")
    y, zh, x, c = r // 16, (r // 8) % 2, (r // 2) % 4, r % 2
    z = zh * 4 + q

    def dev(dy=0, dx=0, dc=0):
        ny, nx, nc = (y + dy) % NY, (x + dx) % NX, (c + dc) % 2
        return (q, ny * 16 + zh * 8 + nx * 2 + nc)

    def dev_z(dz):
        nz = (z + dz) % NZ
        return (nz % 4, y * 16 + (nz // 4) * 8 + x * 2 + c)

    def dev_rep(dq):
        return ((q + dq) % 4, r)

    z_partner = dev_z(4)
    right_y, left_y, right_x, left_x = dev(dy=1), dev(dy=NY - 1), dev(dx=1), dev(dx=NX - 1)
    sibling = dev(dc=1)
    line_y = [dev(dy=j) for j in range(1, NY)]
    line_xc = [(dx, dc, dev(dx=dx, dc=dc)) for dx in range(NX) for dc in range(2) if dx or dc]
    line_z = [dev_z(j) for j in range(1, NZ)]

    barrier = pltpu.get_barrier_semaphore()
    for peer in line_y + [p for _, _, p in line_xc] + line_z:
        pl.semaphore_signal(barrier, inc=1, device_id=peer, device_id_type=MESH)

    load = pltpu.make_async_copy(tiles_hbm, tiles.at[pl.ds(0, SLOTS)], tile_sem)
    load.start()
    tiles[SLOTS] = jnp.zeros((T, T), jnp.bfloat16)

    places = lax.broadcasted_iota(jnp.int32, (T, T), 0) == order[...]
    onehot = places.astype(jnp.float32).astype(jnp.bfloat16)

    def store_own(p, block):
        G[p, 0, pl.ds(row1(0, 0, 0), R1)] = block[:R1]
        G[p, 0, pl.ds(row2(0, 0, 0), R2)] = block[R1:]

    store_own(0, lax.dot_general(
        onehot, features[...], (((0,), (0,)), ((), ())), preferred_element_type=jnp.float32
    ).astype(jnp.bfloat16))
    acc[...] = jnp.zeros_like(acc)

    pl.semaphore_wait(barrier, 21)

    def push(src, dst, send_sem, recv_sem, device):
        pltpu.make_async_remote_copy(
            src_ref=src, dst_ref=dst, send_sem=send_sem, recv_sem=recv_sem,
            device_id=device, device_id_type=MESH,
        ).start()

    def await_ref(ref, sem):
        pltpu.make_async_copy(ref, ref, sem).wait()

    def steps(p):
        own = G.at[p, 0]
        other = G.at[p, 1]

        def go(src, dst, n, kind, sem, device):
            push(own.at[pl.ds(src, n)], own.at[pl.ds(dst, n)], send.at[p, kind], recv.at[p, sem], device)

        def wait(sem, n):
            await_ref(own.at[pl.ds(0, n)], recv.at[p, sem])

        def sib(at, n, ab, g):
            push(own.at[pl.ds(at, n)], other.at[pl.ds(at, n)], send.at[p, SEND_SIB], recv.at[p, sem_sib(ab, g)], sibling)

        def sib1(ab, d):
            sib(row1(ab, d, 0), 4 * R1, ab, (0, 1, 1, 2, 2, 3, 3, 3)[d])

        def sib2(ab, xi, g):
            sib(row2(ab, xi, GROUPS[g][0]), GROUPS[g][1] * R2, ab, g)

        def send_x1(ab):
            for dx, xi in ((1, 1), (3, 2), (2, 3)):
                go(row1(ab, 0, 0), row1(ab, 0, xi), R1, SEND_X1, sem_x1(ab), dev(dx=dx))

        def y1(ab, src, dst, device):
            go(row1(ab, src, 0), row1(ab, dst, 0), 4 * R1, SEND_Y1, sem_y1(ab, dst), device)

        def y2(ab, src, dst, device):
            go(row2(ab, 0, src), row2(ab, 0, dst), R2, SEND_Y2, sem_y2(ab, dst), device)

        def x2(ab, src, dst, g, device):
            d, n = GROUPS[g]
            go(row2(ab, src, d), row2(ab, dst, d), n * R2, SEND_X2, sem_x2(ab, dst, g), device)

        def x2_own(ab, g):
            x2(ab, 0, 1, g, right_x)
            x2(ab, 0, 2, g, left_x)
            sib2(ab, 0, g)

        def x2_pass(ab, g):
            n = GROUPS[g][1] * R2
            wait(sem_x2(ab, 1, g), n)
            if g in (0, 3):
                x2(ab, 1, 3, g, right_x)
            wait(sem_x2(ab, 2, g), n)
            if g in (1, 2):
                x2(ab, 2, 3, g, left_x)
            sib2(ab, 1, g)
            sib2(ab, 2, g)

        def x2_last(ab, g):
            wait(sem_x2(ab, 3, g), GROUPS[g][1] * R2)
            sib2(ab, 3, g)

        def ring_pass(ab, hop, sem, move, n, after):
            lo, hi = 2 * hop - 1, 2 * hop
            wait(sem(ab, lo), n)
            if hop < 3:
                move(ab, lo, lo + 2, right_y)
            elif ab == 0:
                move(ab, lo, 7, right_y)
            wait(sem(ab, hi), n)
            if hop < 3:
                move(ab, hi, hi + 2, left_y)
            elif ab == 1:
                move(ab, hi, 7, left_y)
            if after:
                sib1(ab, lo)
                sib1(ab, hi)

        def y1_pass(ab, hop):
            ring_pass(ab, hop, sem_y1, y1, 4 * R1, True)

        def y2_pass(ab, hop):
            ring_pass(ab, hop, sem_y2, y2, R2, False)

        def compute(ab, g):
            d0, n = GROUPS[g]
            await_ref(other.at[pl.ds(0, n * 512)], recv.at[p, sem_sib(ab, g)])

            def body(i, carry):
                d, k = d0 + i // 2, i % 2
                base = (ab * 8 + d) * 32 + k * 4
                left = jnp.concatenate([
                    jnp.concatenate([tiles[table[base + xi * 8 + j]] for xi in range(4)], axis=1)
                    for j in range(4)
                ], axis=0)
                pieces = []
                for xi in range(4):
                    pieces.append(G[p, k, pl.ds(pl.multiple_of(row1(ab, d, xi), R1), R1)])
                    pieces.append(G[p, k, pl.ds(pl.multiple_of(row2(ab, xi, d), R2), R2)])
                right = jnp.concatenate(pieces, axis=0)
                acc[...] += jnp.dot(left, right, preferred_element_type=jnp.float32)
                return carry

            lax.fori_loop(0, 2 * n, body, 0)

        def s0(ab):
            if ab == 1:
                wait(SEM_Z, R1 + R2)
            send_x1(ab)
            y2(ab, 0, 1, right_y)
            y2(ab, 0, 2, left_y)
            if ab == 0:
                for at, n in ((row1(0, 0, 0), R1), (row2(0, 0, 0), R2)):
                    dst = row1(1, 0, 0) if n == R1 and at == row1(0, 0, 0) else row2(1, 0, 0)
                    go(at, dst, n, SEND_Z, SEM_Z, z_partner)
            x2_own(ab, 0)

        def s1(ab):
            wait(sem_x1(ab), 3 * R1)
            y1(ab, 0, 1, right_y)
            y1(ab, 0, 2, left_y)
            sib1(ab, 0)

        def s2(ab):
            y2_pass(ab, 1)
            x2_own(ab, 1)

        def s3(ab):
            x2_pass(ab, 0)

        def s4(ab):
            y2_pass(ab, 2)
            x2_own(ab, 2)

        def s5(ab):
            y1_pass(ab, 1)

        def s6(ab):
            x2_pass(ab, 1)

        def s7(ab):
            y2_pass(ab, 3)

        def s8(ab):
            wait(sem_y2(ab, 7), R2)
            x2_own(ab, 3)

        def s9(ab):
            x2_last(ab, 0)

        def s10(ab):
            y1_pass(ab, 2)

        def s11(ab):
            x2_pass(ab, 2)

        def s12(ab):
            x2_last(ab, 1)

        def s13(ab):
            y1_pass(ab, 3)

        def s14(ab):
            x2_pass(ab, 3)

        def s15(ab):
            x2_last(ab, 2)

        def s16(ab):
            wait(sem_y1(ab, 7), 4 * R1)
            sib1(ab, 7)

        def s17(ab):
            x2_last(ab, 3)

        def finish():
            for kind, n in ((SEND_Z, R1 + R2), (SEND_X1, 6 * R1), (SEND_Y1, 56 * R1), (SEND_Y2, 14 * R2), (SEND_X2, 48 * R2), (SEND_SIB, ROWS)):
                await_ref(own.at[pl.ds(0, n)], send.at[p, kind])

        table_of = {f"s{i}": f for i, f in enumerate(
            (s0, s1, s2, s3, s4, s5, s6, s7, s8, s9, s10, s11, s12, s13, s14, s15, s16, s17))}
        for g in range(4):
            table_of[f"c{g}"] = functools.partial(lambda g, ab: compute(ab, g), g)
        return table_of, finish

    PLAN = (
        "a s0 s1 s2 s3 b s0 a s4 s5 b s1 a s6 s7 b s2 a s8 s9 c0 b s3 a s10 b s4 a s11 s12 c1 b s5 a s13 b s6 s7"
        " a s14 s15 c2 b s8 s9 c0 a s16 s17 c3 b s10 s11 s12 c1 s13 s14 s15 c2 s16 s17 c3"
    ).split()

    def run(p, extra):
        table_of, finish = steps(p)
        ab = 0
        for at, word in enumerate(PLAN):
            if word in ("a", "b"):
                ab = "ab".index(word)
                continue
            table_of[word](ab)
            for f in extra.get(("ab"[ab], word), ()):
                f()
        return finish

    def reduce_rep(p):
        for j in range(1, 4):
            part[p, j - 1] = acc[pl.ds(j * T, T)].astype(jnp.bfloat16)
        for j in range(1, 4):
            push(part.at[p, j - 1], part_in.at[p, j - 1], rs_send.at[p], rs_recv.at[p], dev_rep(j))
        await_ref(part_in.at[p], rs_recv.at[p])
        total = acc[pl.ds(0, T)]
        for j in range(3):
            total = total + part_in[p, j].astype(jnp.float32)
        return total

    finish0 = run(0, {("a", "s3"): (load.wait,)})
    hidden = reduce_rep(0).astype(jnp.bfloat16)
    pre_act = jnp.dot(hidden, weight[...], preferred_element_type=jnp.float32) + bias[...]
    gate = jax.nn.sigmoid(pre_act)
    pre_grad = (cotangent[...].astype(jnp.float32) * gate * (1.0 + pre_act * (1.0 - gate))).astype(jnp.bfloat16)
    store_own(1, lax.dot_general(
        pre_grad, weight[...], (((1,), (1,)), ((), ())), preferred_element_type=jnp.float32
    ).astype(jnp.bfloat16))
    acc[...] = jnp.zeros_like(acc)

    def terms():
        act_out[...] = (pre_act * gate).astype(jnp.bfloat16)
        weight_term = lax.dot_general(
            hidden, pre_grad, (((0,), (0,)), ((), ())), preferred_element_type=jnp.float32
        )
        bias_term = jnp.sum(pre_grad.astype(jnp.float32), axis=0, keepdims=True)
        rows = lax.broadcasted_iota(jnp.int32, (8, T), 0)
        bias_tile = jnp.where(rows == 0, bias_term[:, :T], jnp.where(rows == 1, bias_term[:, T:], 0.0))
        for piece in range(NZ):
            for t in range(4):
                wp[piece, t] = weight_term[piece * 16 + (t // 2) * 8:piece * 16 + (t // 2) * 8 + 8, (t % 2) * T:(t % 2) * T + T]
            wp[piece, 4] = bias_tile

    def ar1():
        for j in range(1, NZ):
            push(wp.at[(z + j) % NZ], wp_in.at[j - 1], ar_send.at[0], ar_recv.at[0], dev_z(j))

    def ar2():
        await_ref(wp_in, ar_recv.at[0])
        total = wp[z]
        for j in range(NZ - 1):
            total = total + wp_in[j]
        for t in range(4):
            w2[t, 0] = total[t]
            w2[t, 1] = total[4]
        for dx, dc, device in line_xc:
            push(w2.at[(x + dx) % NX], w2_in.at[((NX - dx) % NX) * 2 + dc - 1], ar_send.at[1], ar_recv.at[1], device)

    def ar3():
        await_ref(w2_in, ar_recv.at[1])
        total = w2[x]
        for j in range(7):
            total = total + w2_in[j]
        w3[...] = total
        for j in range(1, NY):
            push(w3, w3_in.at[j - 1], ar_send.at[2], ar_recv.at[2], dev(dy=j))

    def ar4():
        await_ref(w3_in, ar_recv.at[2])
        total = w3[...]
        for j in range(NY - 1):
            total = total + w3_in[j]
        bgrad_out[...] = total[1]
        wq[x] = total[0]
        for dx in range(1, NX):
            push(wq.at[x], wq.at[x], ar_send.at[3], ar_recv.at[3], dev(dx=dx))

    def ar5():
        await_ref(wq.at[pl.ds(0, NX - 1)], ar_recv.at[3])
        wfull[z] = wq[...]
        for j in range(1, NZ):
            push(wfull.at[z], wfull.at[z], ar_send.at[4], ar_recv.at[4], dev_z(j))

    finish1 = run(1, {
        ("a", "s0"): (terms,), ("b", "s2"): (ar1,), ("b", "s4"): (ar2,), ("b", "s7"): (ar3,), ("a", "c3"): (ar4,), ("b", "s12"): (ar5,),
    })
    total = reduce_rep(1)
    grad = None
    for _ in range(3):
        piece = total.astype(jnp.bfloat16)
        total = total - piece.astype(jnp.float32)
        moved = jnp.dot(onehot, piece, preferred_element_type=jnp.float32)
        grad = moved if grad is None else grad + moved
    fgrad_out[...] = grad

    await_ref(wfull.at[pl.ds(0, NZ - 1)], ar_recv.at[4])
    for piece in range(NZ):
        for t in range(4):
            wgrad_out[pl.ds(piece * 16 + (t // 2) * 8, 8), pl.ds((t % 2) * T, T)] = wfull[piece, t]

    finish0()
    finish1()
    for p in range(2):
        await_ref(part.at[p], rs_send.at[p])
    await_ref(wp.at[pl.ds(0, NZ - 1)], ar_send.at[0])
    await_ref(w2_in, ar_send.at[1])
    await_ref(w3_in, ar_send.at[2])
    await_ref(wq.at[pl.ds(0, NX - 1)], ar_send.at[3])
    await_ref(wfull.at[pl.ds(0, NZ - 1)], ar_send.at[4])


def slot_table(tile_row, tile_col, tile_count):
    q = lax.axis_index("rep")
    r = lax.axis_index("row")
    y, zh, x, c = r // 16, (r // 8) % 2, (r // 2) % 4, r % 2
    place = jnp.arange(512, dtype=jnp.int32)
    j, k, xi, d, ab = place % 4, (place // 4) % 2, (place // 8) % 4, (place // 32) % 8, place // 256
    dy = jnp.where(d == 7, 4, jnp.where(d % 2 == 1, -((d + 1) // 2), d // 2))
    dx = jnp.where(xi == 3, 2, jnp.where(xi == 1, -1, xi // 2))
    col = ((y + dy) % NY) * 16 + (zh + ab) % 2 * 8 + ((x + dx) % NX) * 2 + (c + k) % 2
    want = col * 4 + (q + j) % 4
    have = tile_col.reshape(SLOTS) * 4 + tile_row.reshape(SLOTS)
    slots = jnp.arange(SLOTS, dtype=jnp.int32)
    hit = (want[:, None] == have[None, :]) & (slots[None, :] < tile_count.reshape(1, 1))
    return jnp.min(jnp.where(hit, slots[None, :], SLOTS), axis=1)


def local(
    features, node_order, tile_values, tile_row, tile_col, tile_count, weight, bias_vec, cotangent
):
    table = slot_table(tile_row, tile_col, tile_count)
    vmem = pl.BlockSpec(memory_space=pltpu.VMEM)
    act, fgrad, wgrad, bgrad = pl.pallas_call(
        kernel,
        out_shape=(
            jax.ShapeDtypeStruct((T, 256), jnp.bfloat16),
            jax.ShapeDtypeStruct((T, T), jnp.float32),
            jax.ShapeDtypeStruct((T, 256), jnp.float32),
            jax.ShapeDtypeStruct((8, T), jnp.float32),
        ),
        in_specs=[
            vmem, vmem, pl.BlockSpec(memory_space=pl.ANY), pl.BlockSpec(memory_space=pltpu.SMEM), vmem, vmem, vmem,
        ],
        out_specs=(vmem, vmem, vmem, vmem),
        scratch_shapes=[
            pltpu.VMEM((SLOTS + 1, T, T), jnp.bfloat16),
            pltpu.VMEM((2, 2, ROWS, T), jnp.bfloat16),
            pltpu.VMEM((4 * T, T), jnp.float32),
            pltpu.VMEM((2, 3, T, T), jnp.bfloat16),
            pltpu.VMEM((2, 3, T, T), jnp.bfloat16),
            pltpu.VMEM((NZ, 5, 8, T), jnp.float32),
            pltpu.VMEM((NZ - 1, 5, 8, T), jnp.float32),
            pltpu.VMEM((NX, 2, 8, T), jnp.float32),
            pltpu.VMEM((7, 2, 8, T), jnp.float32),
            pltpu.VMEM((2, 8, T), jnp.float32),
            pltpu.VMEM((NY - 1, 2, 8, T), jnp.float32),
            pltpu.VMEM((NX, 8, T), jnp.float32),
            pltpu.VMEM((NZ, 4, 8, T), jnp.float32),
            pltpu.SemaphoreType.DMA,
            pltpu.SemaphoreType.DMA((2, N_RECV)),
            pltpu.SemaphoreType.DMA((2, 6)),
            pltpu.SemaphoreType.DMA((2,)),
            pltpu.SemaphoreType.DMA((2,)),
            pltpu.SemaphoreType.DMA((5,)),
            pltpu.SemaphoreType.DMA((5,)),
        ],
        compiler_params=pltpu.CompilerParams(
            collective_id=0, has_side_effects=True, vmem_limit_bytes=48 * 1024 * 1024
        ),
    )(
        features, node_order, tile_values.reshape(SLOTS, T, T), table, weight, bias_vec.reshape(1, 256), cotangent
    )
    return act, fgrad, wgrad, bgrad[:2].reshape(256)


def solution(mesh):
    return jax.shard_map(
        local,
        mesh=mesh,
        in_specs=(
            P(("rep", "row"), None),
            P(("rep", "row"), None),
            P("rep", "row", None, None, None),
            P("rep", "row", None),
            P("rep", "row", None),
            P("rep", "row"),
            P(),
            P(),
            P(("rep", "row"), None),
        ),
        out_specs=(P(("rep", "row"), None), P(("rep", "row"), None), P(), P()),
        check_vma=False,
    )
```

time: 679 us -> 111 us (0.16)
  waiting for transfers between devices: 497 us -> 0 us
  Pallas kernels: 0 us -> 99.9 us
  blocking collectives: 97.1 us -> 0 us
  local copies, waits for them, and re-layouts: 40 us -> 8.49 us
  matrix products: 27.2 us -> 0 us
  between operations: 14.5 us -> 1.38 us
    all_gather x2 -> x0, waiting for transfers between devices: 291 us -> none  [the longest x1 147 us: local(): gathered = lax.all_gather(permuted, 'row', axis=0, tiled=True)]
    psum x1 -> x0, waiting for transfers between devices: 187 us -> none  [local(): weight_grad, bias_grad = lax.psum((weight_term, bias_term), ('rep', 'row'))]
    pallas_call x0 -> x1, Pallas kernels: none -> 99.9 us  [local(): pl.pallas_call(kernel, out_shape=(jax.ShapeDtypeStruct((T, 256), jnp.bflo...]
    psum x1 -> x0, blocking collectives: 97.1 us -> none  [local(): weight_grad, bias_grad = lax.psum((weight_term, bias_term), ('rep', 'row'))]
    dot_general x7 -> x0, matrix products: 27.2 us -> none  [the longest x2 17.9 us: combine_tiles(): jnp.einsum('kab,kbw->kaw', tile_mats, picked, preferred_element_type=jnp....]
    gather x3 -> x0, local copies, waits for them, and re-layouts: 21.4 us -> none  [the longest x2 19.4 us: combine_tiles(): picked = blocks[col_slot]]
    reduce_scatter x2 -> x0, waiting for transfers between devices: 19.4 us -> none  [the longest x1 19.4 us: local(): lax.psum_scatter(partial_value, 'rep', scatter_dimension=0, tiled=True)]
    dot_general x4 -> x0, local copies, waits for them, and re-layouts: 15.2 us -> none  [the longest x2 13.8 us: combine_tiles(): jnp.einsum('kab,kbw->kaw', tile_mats, picked, preferred_element_type=jnp....]
  transfers between devices with their start and end apart: 5 -> 0, of which waited for: 4 -> 0; matrix products, arithmetic and copies ran while one was open for 0% -> 0% of each run, Pallas kernels for 0% -> 0%
where the time goes in v1:
time: 111 us
  Pallas kernels  99.9 us (90%)
  local copies, waits for them, and re-layouts  8.49 us (8%)
  between operations  1.38 us (1%)
    pallas_call x1, Pallas kernels, local(): pl.pallas_call(kernel, out_shape=(jax.ShapeDtypeStruct((T, 256), jnp.bflo...  99.9 us
    unnamed x15, local copies, waits for them, and re-layouts  7.93 us

profile of v1, /device:TPU:1, one launch (start us, length us, event | category | flops | bytes accessed | tf_op | source)
XLA Modules:
  0.0 110.6 jit_solution(13641881696489731099)
XLA Ops:
  1.4 0.7 multiply_add_fusion
  2.1 0.1 select_reduce_fusion.table
  2.2 0.0 copy-start
  2.2 2.2 %copy-done = bf16[1,1,135,128,128]{4,3,2,1,0:T(8,128)(2,1)S(1)} copy-done((bf16[1,1,135,128,128]{4,3,2,1,0:T(8,128)(2,1)S(1)}, bf16[1,1,135,128,128]{4,3,2,1,0:T(8,128)(2,1)}, u32[]{:S(2)}) %copy-start) | copy-done | bytes 4423704
  4.5 0.0 copy-start.1
  4.5 0.8 copy-done.1
  5.3 0.0 copy-start.2
  5.3 0.8 copy-done.2
  6.2 0.0 copy-start.3
  6.2 0.8 copy-done.3
  6.9 0.0 copy-start.4
  6.9 0.7 copy-done.4
  7.6 0.0 copy-start.5
  7.6 0.7 copy-done.5
  8.3 99.9 %shard_map.120 = (bf16[128,256]{1,0:T(8,128)(2,1)S(1)}, f32[128,128]{1,0:T(8,128)S(1)}, f32[128,256]{1,0:T(8,128)S(1)}, f32[8,128]{1,0:T(8,128)S(1)}) custom-call(bf16[128,128]{1,0:T(8,128)(2,1)S(1)} %copy-done.3, s32[1,128]{1,0:T(1,128)S(1)} %copy-done.5, bf16[135,128,128]{2,1,0:T(8,128)(2,1)S(1)} %bitcast.7, s32[512]{0:T(512)S(1)} %select_reduce_fusion.table, ...), custom_call_target="tpu_custom_call" | custom-call | tf_op jit(solution)/shard_map/pallas_call | solution.py:432
  108.1 0.6 slice_bitcast_fusion
  108.7 0.6 copy.17
  109.3 0.6 copy.18
  110.0 0.7 copy.19
  (2 shorter events, 0.0 us)
Async XLA Ops:
  2.2 2.3 %copy-start = (bf16[1,1,135,128,128]{4,3,2,1,0:T(8,128)(2,1)S(1)}, bf16[1,1,135,128,128]{4,3,2,1,0:T(8,128)(2,1)}, u32[]{:S(2)}) copy-start(bf16[1,1,135,128,128]{4,3,2,1,0:T(8,128)(2,1)} %param.11) | copy-start | bytes 13271044
  4.5 0.8 copy-start.1
  5.3 0.8 copy-start.2
  6.2 0.8 copy-start.3
  6.9 0.7 copy-start.4
  7.6 0.7 copy-start.5

commit v2 on v1

v2 whole, which is shorter than its diff:
```python
import functools

import jax
import jax.numpy as jnp
from jax import lax
from jax.experimental import pallas as pl
from jax.experimental.pallas import tpu as pltpu
from jax.sharding import PartitionSpec as P

MESH = pl.DeviceIdType.MESH
NX, NY, NZ = 4, 8, 8
T = 128
R1, R2 = 32, 96
SLOTS = 135
GROUPS = ((0, 1), (1, 4), (5, 3))
GROUP_OF = (0, 1, 1, 1, 1, 2, 2, 2)
DIRECT = ()
ROWS = 64 * (R1 + R2)


def row1(ab, d, xi):
    return ((ab * 8 + d) * 4 + xi) * R1


def row2(ab, xi, d):
    return 64 * R1 + ((ab * 4 + xi) * 8 + d) * R2


PLAN = (
    (0, "z"), (0, "y2s"), (0, "o0"), (2, "ar1"), (0, "x1s"), (0, "pl0"), (0, "y2f"), (0, "o1"), (1, "x1s"),
    (1, "y2s"), (0, "y1n1"), (0, "y1n2"), (1, "o0"), (2, "ar2"), (0, "l0"), (0, "o2"), (0, "pl1"), (0, "pr1"),
    (1, "y2f"), (1, "o1"), (0, "pr0"), (1, "pr0"), (1, "y1n2"), (2, "ar3"), (0, "m0"), (0, "pr2"), (0, "pl2"),
    (1, "pl0"), (0, "y1f"), (0, "y1b"), (0, "l1"), (1, "y1n1"), (1, "o2"), (0, "m3"), (1, "pr1"), (1, "pl1"),
    (0, "m1"), (0, "m4"), (1, "y1f"), (1, "l0"), (0, "l2"), (0, "m2"), (0, "y1l"), (2, "ar4"), (1, "pr2"), (1, "y1b"),
    (1, "pl2"), (1, "m0"), (1, "l1"), (0, "m7"), (0, "m5"), (0, "m6"), (1, "m1"), (1, "y1l"), (1, "m2"), (1, "l2"),
    (2, "ar5"), (1, "m3"), (1, "m4"), (1, "m6"), (1, "m7"), (1, "m5"),
)


SEM_Z = 0


def sem_x1(ab):
    return 1 + ab


def sem_y1(ab, step):
    return 3 + ab * 3 + step


def sem_y2(ab, step):
    return 9 + ab * 2 + step


def sem_x2(ab, xi, g):
    return 13 + (ab * 3 + xi - 1) * 3 + g


def sem_sib(ab, g):
    return 31 + ab * 3 + g


N_RECV = 37
SEND_Z, SEND_X1, SEND_Y1, SEND_Y2, SEND_X2, SEND_SIB = range(6)


def kernel(
    features_hbm, order_hbm, tiles_hbm, table, weight_hbm, bias_hbm, cotangent_hbm,
    act_out, fgrad_out, wgrad_out, bgrad_out,
    features, order, weight, bias, cotangent,
    tiles, G, acc, part, part_in, wp, wp_in, w2, w2_in, w3, w3_in, wq, wfull,
    load_sem, recv, send, rs_recv, rs_send, ar_recv, ar_send,
):
    q = lax.axis_index("rep")
    r = lax.axis_index("row")
    y, zh, x, c = r // 16, (r // 8) % 2, (r // 2) % 4, r % 2
    z = zh * 4 + q

    def dev(dy=0, dx=0, dc=0):
        ny, nx, nc = (y + dy) % NY, (x + dx) % NX, (c + dc) % 2
        return (q, ny * 16 + zh * 8 + nx * 2 + nc)

    def dev_z(dz):
        nz = (z + dz) % NZ
        return (nz % 4, y * 16 + (nz // 4) * 8 + x * 2 + c)

    def dev_rep(dq):
        return ((q + dq) % 4, r)

    z_partner = dev_z(4)
    along_y = {j: dev(dy=j % NY) for j in (-2, -1, 1, 2)}
    along_x = {j: dev(dx=j % NX) for j in (-1, 1, 2)}
    sibling = dev(dc=1)
    line_y = [dev(dy=j) for j in range(1, NY)]
    line_xc = [(dx, dc, dev(dx=dx, dc=dc)) for dx in range(NX) for dc in range(2) if dx or dc]
    line_z = [dev_z(j) for j in range(1, NZ)]

    barrier = pltpu.get_barrier_semaphore()
    for peer in line_y + [p for _, _, p in line_xc] + line_z:
        pl.semaphore_signal(barrier, inc=1, device_id=peer, device_id_type=MESH)

    loads = [
        pltpu.make_async_copy(src, dst, load_sem.at[i]) for i, (src, dst) in enumerate((
            (features_hbm, features), (order_hbm, order), (tiles_hbm, tiles.at[pl.ds(0, SLOTS)]),
            (weight_hbm, weight), (bias_hbm, bias), (cotangent_hbm, cotangent),
        ))
    ]
    for load in loads:
        load.start()
    tiles[SLOTS] = jnp.zeros((T, T), jnp.bfloat16)

    acc[...] = jnp.zeros_like(acc)
    loads[0].wait()
    loads[1].wait()
    places = lax.broadcasted_iota(jnp.int32, (T, T), 0) == order[...]
    onehot = places.astype(jnp.float32).astype(jnp.bfloat16)

    def store_own(p, block):
        G[p, 0, pl.ds(row1(0, 0, 0), R1)] = block[:R1]
        G[p, 0, pl.ds(row2(0, 0, 0), R2)] = block[R1:]

    store_own(0, lax.dot_general(
        onehot, features[...], (((0,), (0,)), ((), ())), preferred_element_type=jnp.float32
    ).astype(jnp.bfloat16))

    pl.semaphore_wait(barrier, 21)

    def push(src, dst, send_sem, recv_sem, device):
        pltpu.make_async_remote_copy(
            src_ref=src, dst_ref=dst, send_sem=send_sem, recv_sem=recv_sem,
            device_id=device, device_id_type=MESH,
        ).start()

    def await_ref(ref, sem):
        pltpu.make_async_copy(ref, ref, sem).wait()

    def steps(p):
        own = G.at[p, 0]
        other = G.at[p, 1]
        waited = set()

        def go(src, dst, n, kind, sem, device):
            push(own.at[pl.ds(src, n)], own.at[pl.ds(dst, n)], send.at[p, kind], recv.at[p, sem], device)

        def ensure(sem, n):
            if sem not in waited:
                waited.add(sem)
                await_ref(own.at[pl.ds(0, n)], recv.at[p, sem])

        def sib(at, n, ab, g):
            push(own.at[pl.ds(at, n)], other.at[pl.ds(at, n)], send.at[p, SEND_SIB], recv.at[p, sem_sib(ab, g)], sibling)

        def sib1(ab, d, n, g):
            sib(row1(ab, d, 0), n * 4 * R1, ab, g)

        def sib2(ab, xi, g):
            sib(row2(ab, xi, GROUPS[g][0]), GROUPS[g][1] * R2, ab, g)

        def y1(ab, src, dst, step, dy):
            go(row1(ab, src, 0), row1(ab, dst, 0), 4 * R1, SEND_Y1, sem_y1(ab, step), along_y[dy])

        def y2(ab, src, dst, step, dy):
            go(row2(ab, 0, src), row2(ab, 0, dst), R2, SEND_Y2, sem_y2(ab, step), along_y[dy])

        def x2(ab, src, dst, g, dx, first=0, n=None):
            d, n = GROUPS[g][0] + first, GROUPS[g][1] if n is None else n
            if n:
                go(row2(ab, src, d), row2(ab, dst, d), n * R2, SEND_X2, sem_x2(ab, dst, g), along_x[dx])

        def own_ready(ab):
            if ab == 1:
                ensure(SEM_Z, R1 + R2)

        def partner():
            go(row1(0, 0, 0), row1(1, 0, 0), R1, SEND_Z, SEM_Z, z_partner)
            go(row2(0, 0, 0), row2(1, 0, 0), R2, SEND_Z, SEM_Z, z_partner)

        def y2_start(ab):
            own_ready(ab)
            for dst, dy in ((3, 2), (4, -2), (1, 1), (2, -1)):
                y2(ab, 0, dst, 0, dy)

        def x1_start(ab):
            own_ready(ab)
            for dx, xi in ((2, 3), (1, 1), (-1, 2)):
                go(row1(ab, 0, 0), row1(ab, 0, xi), R1, SEND_X1, sem_x1(ab), along_x[dx])

        def x2_own(ab, g):
            if g == 0:
                own_ready(ab)
            else:
                ensure(sem_y2(ab, g - 1), (4, 3)[g - 1] * R2)
            if (ab, g) in DIRECT:
                x2(ab, 0, 3, g, 2)
            x2(ab, 0, 1, g, 1)
            x2(ab, 0, 2, g, -1)
            sib2(ab, 0, g)

        def x2_pass(ab, g, xi):
            n = GROUPS[g][1]
            half = (n + 1 - ab) // 2
            ensure(sem_x2(ab, xi, g), n * R2)
            if (ab, g) not in DIRECT:
                if xi == 1:
                    x2(ab, 1, 3, g, 1, 0, half)
                else:
                    x2(ab, 2, 3, g, -1, half, n - half)
            sib2(ab, xi, g)

        def x2_last(ab, g):
            ensure(sem_x2(ab, 3, g), GROUPS[g][1] * R2)
            sib2(ab, 3, g)

        def y1_two(ab):
            ensure(sem_x1(ab), 3 * R1)
            y1(ab, 0, 3, 1, 2)
            y1(ab, 0, 4, 1, -2)

        def y1_one(ab):
            ensure(sem_x1(ab), 3 * R1)
            y1(ab, 0, 1, 0, 1)
            y1(ab, 0, 2, 0, -1)
            sib1(ab, 0, 1, 0)

        def y1_near(ab):
            ensure(sem_y1(ab, 0), 8 * R1)
            sib1(ab, 1, 2, 1)

        def y1_far(ab):
            ensure(sem_y1(ab, 1), 8 * R1)
            if ab == 0:
                y1(ab, 3, 7, 2, 2)
            else:
                y1(ab, 4, 7, 2, -2)
            y1(ab, 3, 5, 2, 1)
            y1(ab, 4, 6, 2, -1)
            sib1(ab, 3, 2, 1)

        def y1_last(ab):
            ensure(sem_y1(ab, 2), 12 * R1)
            sib1(ab, 5, 3, 2)

        def y2_far(ab):
            ensure(sem_y2(ab, 0), 4 * R2)
            if ab == 0:
                y2(ab, 3, 7, 1, 2)
            else:
                y2(ab, 4, 7, 1, -2)
            y2(ab, 3, 5, 1, 1)
            y2(ab, 4, 6, 1, -1)

        def mul(ab, d):
            g = GROUP_OF[d]
            ensure(sem_sib(ab, g), GROUPS[g][1] * 512)
            base = (ab * 8 + d) * 32
            left = jnp.concatenate([
                jnp.concatenate([tiles[table[base + col * 4 + j]] for col in range(8)], axis=1) for j in range(4)
            ], axis=0)
            pieces = []
            for xi in range(4):
                for k in range(2):
                    pieces.append(G[p, k, pl.ds(row1(ab, d, xi), R1)])
                    pieces.append(G[p, k, pl.ds(row2(ab, xi, d), R2)])
            acc[...] += jnp.dot(left, jnp.concatenate(pieces, axis=0), preferred_element_type=jnp.float32)

        def finish():
            for kind, n in ((SEND_Z, R1 + R2), (SEND_X1, 6 * R1), (SEND_Y1, 56 * R1), (SEND_Y2, 14 * R2), (SEND_X2, 48 * R2), (SEND_SIB, ROWS)):
                await_ref(own.at[pl.ds(0, n)], send.at[p, kind])

        named = {
            "y2s": y2_start, "x1s": x1_start, "y1n2": y1_two, "y1n1": y1_one, "y1b": y1_near, "y1f": y1_far,
            "y1l": y1_last, "y2f": y2_far, "z": lambda ab: partner(),
        }
        for g in range(3):
            named[f"o{g}"] = functools.partial(lambda g, ab: x2_own(ab, g), g)
            named[f"pl{g}"] = functools.partial(lambda g, ab: x2_pass(ab, g, 1), g)
            named[f"pr{g}"] = functools.partial(lambda g, ab: x2_pass(ab, g, 2), g)
            named[f"l{g}"] = functools.partial(lambda g, ab: x2_last(ab, g), g)
        for d in range(8):
            named[f"m{d}"] = functools.partial(lambda d, ab: mul(ab, d), d)
        return named, finish

    def run(p, sums, before_mul):
        named, finish = steps(p)
        for ab, word in PLAN:
            if word[0] == "m":
                before_mul()
            if ab < 2:
                named[word](ab)
            elif sums:
                sums[word]()
        return finish

    def reduce_rep(p):
        for j in range(1, 4):
            part[p, j - 1] = acc[pl.ds(j * T, T)].astype(jnp.bfloat16)
        for j in range(1, 4):
            push(part.at[p, j - 1], part_in.at[p, j - 1], rs_send.at[p], rs_recv.at[p], dev_rep(j))
        await_ref(part_in.at[p], rs_recv.at[p])
        total = acc[pl.ds(0, T)]
        for j in range(3):
            total = total + part_in[p, j].astype(jnp.float32)
        return total

    pending = list(loads[2:])

    def loaded():
        while pending:
            pending.pop().wait()

    finish0 = run(0, None, loaded)
    hidden = reduce_rep(0).astype(jnp.bfloat16)
    pre_act = jnp.dot(hidden, weight[...], preferred_element_type=jnp.float32) + bias[...]
    gate = jax.nn.sigmoid(pre_act)
    pre_grad = (cotangent[...].astype(jnp.float32) * gate * (1.0 + pre_act * (1.0 - gate))).astype(jnp.bfloat16)
    store_own(1, lax.dot_general(
        pre_grad, weight[...], (((1,), (1,)), ((), ())), preferred_element_type=jnp.float32
    ).astype(jnp.bfloat16))
    acc[...] = jnp.zeros_like(acc)

    def terms():
        act_out[...] = (pre_act * gate).astype(jnp.bfloat16)
        weight_term = lax.dot_general(
            hidden, pre_grad, (((0,), (0,)), ((), ())), preferred_element_type=jnp.float32
        )
        bias_term = jnp.sum(pre_grad.astype(jnp.float32), axis=0, keepdims=True)
        rows = lax.broadcasted_iota(jnp.int32, (8, T), 0)
        bias_tile = jnp.where(rows == 0, bias_term[:, :T], jnp.where(rows == 1, bias_term[:, T:], 0.0))
        for piece in range(NZ):
            for t in range(4):
                wp[piece, t] = weight_term[piece * 16 + (t // 2) * 8:piece * 16 + (t // 2) * 8 + 8, (t % 2) * T:(t % 2) * T + T]
            wp[piece, 4] = bias_tile

    def ar1():
        terms()
        for j in (4, 3, 5, 2, 6, 1, 7):
            push(wp.at[(z + j) % NZ], wp_in.at[j - 1], ar_send.at[0], ar_recv.at[0], dev_z(j))

    def ar2():
        await_ref(wp_in, ar_recv.at[0])
        total = wp[z]
        for j in range(NZ - 1):
            total = total + wp_in[j]
        for t in range(4):
            w2[t, 0] = total[t]
            w2[t, 1] = total[4]
        for dx, dc, device in line_xc:
            push(w2.at[(x + dx) % NX], w2_in.at[((NX - dx) % NX) * 2 + dc - 1], ar_send.at[1], ar_recv.at[1], device)

    def ar3():
        await_ref(w2_in, ar_recv.at[1])
        total = w2[x]
        for j in range(7):
            total = total + w2_in[j]
        w3[...] = total
        for j, device in enumerate(line_y):
            push(w3, w3_in.at[j], ar_send.at[2], ar_recv.at[2], device)

    def ar4():
        await_ref(w3_in, ar_recv.at[2])
        total = w3[...]
        for j in range(NY - 1):
            total = total + w3_in[j]
        bgrad_out[...] = total[1]
        wq[x] = total[0]
        for dx in range(1, NX):
            push(wq.at[x], wq.at[x], ar_send.at[3], ar_recv.at[3], dev(dx=dx))

    def ar5():
        await_ref(wq.at[pl.ds(0, NX - 1)], ar_recv.at[3])
        wfull[z] = wq[...]
        for j in (4, 3, 5, 2, 6, 1, 7):
            push(wfull.at[z], wfull.at[z], ar_send.at[4], ar_recv.at[4], dev_z(j))

    finish1 = run(1, {"ar1": ar1, "ar2": ar2, "ar3": ar3, "ar4": ar4, "ar5": ar5}, lambda: None)
    total = reduce_rep(1)
    grad = None
    for _ in range(3):
        piece = total.astype(jnp.bfloat16)
        total = total - piece.astype(jnp.float32)
        moved = jnp.dot(onehot, piece, preferred_element_type=jnp.float32)
        grad = moved if grad is None else grad + moved
    fgrad_out[...] = grad

    await_ref(wfull.at[pl.ds(0, NZ - 1)], ar_recv.at[4])
    for piece in range(8):
        for t in range(4):
            wgrad_out[pl.ds(piece * 16 + (t // 2) * 8, 8), pl.ds((t % 2) * T, T)] = wfull[piece, t]

    finish0()
    finish1()
    for p in range(2):
        await_ref(part.at[p], rs_send.at[p])
    await_ref(wp_in, ar_send.at[0])
    await_ref(w2_in, ar_send.at[1])
    await_ref(w3_in, ar_send.at[2])
    await_ref(wq.at[pl.ds(0, NX - 1)], ar_send.at[3])
    await_ref(wfull.at[pl.ds(0, NZ - 1)], ar_send.at[4])


def slot_table(tile_row, tile_col, tile_count):
    q = lax.axis_index("rep")
    r = lax.axis_index("row")
    y, zh, x, c = r // 16, (r // 8) % 2, (r // 2) % 4, r % 2
    place = jnp.arange(512, dtype=jnp.int32)
    j, k, xi, d, ab = place % 4, (place // 4) % 2, (place // 8) % 4, (place // 32) % 8, place // 256
    dy = jnp.where(d == 7, 4, jnp.where(d % 2 == 1, -((d + 1) // 2), d // 2))
    dx = jnp.where(xi == 3, 2, jnp.where(xi == 1, -1, xi // 2))
    col = ((y + dy) % NY) * 16 + (zh + ab) % 2 * 8 + ((x + dx) % NX) * 2 + (c + k) % 2
    want = col * 4 + (q + j) % 4
    have = tile_col.reshape(SLOTS) * 4 + tile_row.reshape(SLOTS)
    slots = jnp.arange(SLOTS, dtype=jnp.int32)
    hit = (want[:, None] == have[None, :]) & (slots[None, :] < tile_count.reshape(1, 1))
    return jnp.min(jnp.where(hit, slots[None, :], SLOTS), axis=1)


def local(
    features, node_order, tile_values, tile_row, tile_col, tile_count, weight, bias_vec, cotangent
):
    table = slot_table(tile_row, tile_col, tile_count)
    vmem = pl.BlockSpec(memory_space=pltpu.VMEM)
    hbm = pl.BlockSpec(memory_space=pl.ANY)
    act, fgrad, wgrad, bgrad = pl.pallas_call(
        kernel,
        out_shape=(
            jax.ShapeDtypeStruct((T, 256), jnp.bfloat16),
            jax.ShapeDtypeStruct((T, T), jnp.float32),
            jax.ShapeDtypeStruct((T, 256), jnp.float32),
            jax.ShapeDtypeStruct((8, T), jnp.float32),
        ),
        in_specs=[hbm, hbm, hbm, pl.BlockSpec(memory_space=pltpu.SMEM), hbm, hbm, hbm],
        out_specs=(vmem, vmem, vmem, vmem),
        scratch_shapes=[
            pltpu.VMEM((T, T), jnp.bfloat16),
            pltpu.VMEM((1, T), jnp.int32),
            pltpu.VMEM((T, 256), jnp.bfloat16),
            pltpu.VMEM((1, 256), jnp.float32),
            pltpu.VMEM((T, 256), jnp.bfloat16),
            pltpu.VMEM((SLOTS + 1, T, T), jnp.bfloat16),
            pltpu.VMEM((2, 2, ROWS, T), jnp.bfloat16),
            pltpu.VMEM((4 * T, T), jnp.float32),
            pltpu.VMEM((2, 3, T, T), jnp.bfloat16),
            pltpu.VMEM((2, 3, T, T), jnp.bfloat16),
            pltpu.VMEM((8, 5, 8, T), jnp.float32),
            pltpu.VMEM((NZ - 1, 5, 8, T), jnp.float32),
            pltpu.VMEM((NX, 2, 8, T), jnp.float32),
            pltpu.VMEM((7, 2, 8, T), jnp.float32),
            pltpu.VMEM((2, 8, T), jnp.float32),
            pltpu.VMEM((NY - 1, 2, 8, T), jnp.float32),
            pltpu.VMEM((NX, 8, T), jnp.float32),
            pltpu.VMEM((NZ, 4, 8, T), jnp.float32),
            pltpu.SemaphoreType.DMA((6,)),
            pltpu.SemaphoreType.DMA((2, N_RECV)),
            pltpu.SemaphoreType.DMA((2, 6)),
            pltpu.SemaphoreType.DMA((2,)),
            pltpu.SemaphoreType.DMA((2,)),
            pltpu.SemaphoreType.DMA((5,)),
            pltpu.SemaphoreType.DMA((5,)),
        ],
        compiler_params=pltpu.CompilerParams(
            collective_id=0, has_side_effects=True, vmem_limit_bytes=60 * 1024 * 1024
        ),
    )(
        features, node_order, tile_values.reshape(SLOTS, T, T), table, weight, bias_vec.reshape(1, 256), cotangent
    )
    return act, fgrad, wgrad, bgrad[:2].reshape(256)


def solution(mesh):
    return jax.shard_map(
        local,
        mesh=mesh,
        in_specs=(
            P(("rep", "row"), None),
            P(("rep", "row"), None),
            P("rep", "row", None, None, None),
            P("rep", "row", None),
            P("rep", "row", None),
            P("rep", "row"),
            P(),
            P(),
            P(("rep", "row"), None),
        ),
        out_specs=(P(("rep", "row"), None), P(("rep", "row"), None), P(), P()),
        check_vma=False,
    )
```

time: 111 us -> 86.6 us (0.78)
  Pallas kernels: 99.9 us -> 77.7 us
  local copies, waits for them, and re-layouts: 8.49 us -> 5.75 us
    pallas_call x1, Pallas kernels: 99.9 us -> 77.7 us  [local(): pl.pallas_call(kernel, out_shape=(jax.ShapeDtypeStruct((T, 256), jnp.bflo...]
    unnamed x15 -> x3, local copies, waits for them, and re-layouts: 7.93 us -> 4.51 us
where the time goes in v2:
time: 86.6 us; the launch traced here: 86.3 us
  Pallas kernels  77.7 us (90%)
  local copies, waits for them, and re-layouts  5.75 us (7%)
  other arithmetic  1.46 us (2%)
  between operations  1.36 us (2%)
    pallas_call x1, Pallas kernels, local(): pl.pallas_call(kernel, out_shape=(jax.ShapeDtypeStruct((T, 256), jnp.bflo...  77.7 us
    unnamed x3, local copies, waits for them, and re-layouts  4.51 us

profile of v2, /device:TPU:1, one launch (start us, length us, event | category | flops | bytes accessed | tf_op | source)
XLA Modules:
  0.0 86.3 jit_solution(3230091693166741344)
XLA Ops:
  1.4 0.7 multiply_add_fusion
  2.1 0.7 select_reduce_fusion.table
  2.8 77.7 %shard_map.120 = (bf16[128,256]{1,0:T(8,128)(2,1)}, f32[128,128]{1,0:T(8,128)}, f32[128,256]{1,0:T(8,128)}, f32[8,128]{1,0:T(8,128)}) custom-call(bf16[128,128]{1,0:T(8,128)(2,1)} %features_hbm.1, s32[1,128]{1,0:T(1,128)} %order_hbm.1, bf16[135,128,128]{2,1,0:T(8,128)(2,1)} %bitcast.7, s32[512]{0:T(512)} %select_reduce_fusion.table, ...), custom_call_target="tpu_custom_call" | custom-call | tf_op jit(solution)/shard_map/pallas_call | solution.py:423
  80.5 1.2 %slice_bitcast_fusion = f32[256]{0:T(256)} fusion(f32[8,128]{1,0:T(8,128)} %get-tuple-element.11), kind=kLoop, calls=%fused_computation.98 | loop fusion | bytes 2048 | tf_op jit(solution)/shard_map/reshape | solution.py:466
  81.8 1.5 %copy.17 = bf16[128,256]{1,0:T(8,128)(2,1)} copy(bf16[128,256]{1,0:T(8,128)(2,1)} %get-tuple-element.16) | data formatting | bytes 131072
  83.2 1.5 %copy.18 = f32[128,128]{1,0:T(8,128)} copy(f32[128,128]{1,0:T(8,128)} %get-tuple-element.17) | data formatting | bytes 131072
  84.7 1.6 %copy.19 = f32[128,256]{1,0:T(8,128)} copy(f32[128,256]{1,0:T(8,128)} %get-tuple-element.18) | data formatting | bytes 262144
  (2 shorter events, 0.0 us)

commit v3 on v2

--- a/solution.py
+++ b/solution.py
@@ -65,11 +65,11 @@
 
 
 def kernel(
-    features_hbm, order_hbm, tiles_hbm, table, weight_hbm, bias_hbm, cotangent_hbm,
+    features_hbm, order_hbm, tiles_hbm, row_hbm, col_hbm, count_hbm, weight_hbm, bias_hbm, cotangent_hbm,
     act_out, fgrad_out, wgrad_out, bgrad_out,
-    features, order, weight, bias, cotangent,
+    features, order, weight, bias, cotangent, tile_row, tile_col, tile_count, found, table,
     tiles, G, acc, part, part_in, wp, wp_in, w2, w2_in, w3, w3_in, wq, wfull,
-    load_sem, recv, send, rs_recv, rs_send, ar_recv, ar_send,
+    load_sem, fill_sem, recv, send, rs_recv, rs_send, ar_recv, ar_send,
 ):
     q = lax.axis_index("rep")
     r = lax.axis_index("row")
@@ -101,8 +101,8 @@
 
     loads = [
         pltpu.make_async_copy(src, dst, load_sem.at[i]) for i, (src, dst) in enumerate((
-            (features_hbm, features), (order_hbm, order), (tiles_hbm, tiles.at[pl.ds(0, SLOTS)]),
-            (weight_hbm, weight), (bias_hbm, bias), (cotangent_hbm, cotangent),
+            (row_hbm, tile_row), (col_hbm, tile_col), (count_hbm, tile_count), (features_hbm, features), (order_hbm, order),
+            (tiles_hbm, tiles.at[pl.ds(0, SLOTS)]), (weight_hbm, weight), (bias_hbm, bias), (cotangent_hbm, cotangent),
         ))
     ]
     for load in loads:
@@ -110,8 +110,8 @@
     tiles[SLOTS] = jnp.zeros((T, T), jnp.bfloat16)
 
     acc[...] = jnp.zeros_like(acc)
-    loads[0].wait()
-    loads[1].wait()
+    for load in loads[:5]:
+        load.wait()
     places = lax.broadcasted_iota(jnp.int32, (T, T), 0) == order[...]
     onehot = places.astype(jnp.float32).astype(jnp.bfloat16)
 
@@ -122,6 +122,22 @@
     store_own(0, lax.dot_general(
         onehot, features[...], (((0,), (0,)), ((), ())), preferred_element_type=jnp.float32
     ).astype(jnp.bfloat16))
+
+    place = lax.broadcasted_iota(jnp.int32, (4, T), 0) * T + lax.broadcasted_iota(jnp.int32, (4, T), 1)
+    j, k, xi, d, ab = place & 3, (place >> 2) & 1, (place >> 3) & 3, (place >> 5) & 7, place >> 8
+    dy = jnp.where(d == 7, 4, jnp.where((d & 1) == 1, -((d + 1) >> 1), d >> 1))
+    dx = jnp.where(xi == 3, 2, jnp.where(xi == 1, -1, xi >> 1))
+    column = ((y + dy) & 7) * 16 + ((zh + ab) & 1) * 8 + ((x + dx) & 3) * 2 + ((c + k) & 1)
+    want = column * 4 + ((q + j) & 3)
+    used = tile_count[0, 0]
+
+    def look(slot, at):
+        key = jnp.where(slot < used, tile_col[0, slot] * 4 + tile_row[0, slot], -1)
+        return jnp.where(want == key, slot, at)
+
+    found[...] = lax.fori_loop(0, SLOTS, look, jnp.full((4, T), SLOTS, jnp.int32), unroll=5)
+    fill = pltpu.make_async_copy(found, table, fill_sem)
+    fill.start()
 
     pl.semaphore_wait(barrier, 21)
 
@@ -254,7 +270,7 @@
             ensure(sem_sib(ab, g), GROUPS[g][1] * 512)
             base = (ab * 8 + d) * 32
             left = jnp.concatenate([
-                jnp.concatenate([tiles[table[base + col * 4 + j]] for col in range(8)], axis=1) for j in range(4)
+                jnp.concatenate([tiles[table[(base + col * 4 + j) // T, (base + col * 4 + j) % T]] for col in range(8)], axis=1) for j in range(4)
             ], axis=0)
             pieces = []
             for xi in range(4):
@@ -294,7 +310,7 @@
     def reduce_rep(p):
         for j in range(1, 4):
             part[p, j - 1] = acc[pl.ds(j * T, T)].astype(jnp.bfloat16)
-        for j in range(1, 4):
+        for j in (3, 2, 1):
             push(part.at[p, j - 1], part_in.at[p, j - 1], rs_send.at[p], rs_recv.at[p], dev_rep(j))
         await_ref(part_in.at[p], rs_recv.at[p])
         total = acc[pl.ds(0, T)]
@@ -302,7 +318,7 @@
             total = total + part_in[p, j].astype(jnp.float32)
         return total
 
-    pending = list(loads[2:])
+    pending = [fill] + loads[5:]
 
     def loaded():
         while pending:
@@ -361,7 +377,8 @@
         total = w3[...]
         for j in range(NY - 1):
             total = total + w3_in[j]
-        bgrad_out[...] = total[1]
+        bgrad_out[:, :T] = total[1, 0:1]
+        bgrad_out[:, T:] = total[1, 1:2]
         wq[x] = total[0]
         for dx in range(1, NX):
             push(wq.at[x], wq.at[x], ar_send.at[3], ar_recv.at[3], dev(dx=dx))
@@ -398,26 +415,22 @@
     await_ref(wfull.at[pl.ds(0, NZ - 1)], ar_send.at[4])
 
 
-def slot_table(tile_row, tile_col, tile_count):
-    q = lax.axis_index("rep")
-    r = lax.axis_index("row")
-    y, zh, x, c = r // 16, (r // 8) % 2, (r // 2) % 4, r % 2
-    place = jnp.arange(512, dtype=jnp.int32)
-    j, k, xi, d, ab = place % 4, (place // 4) % 2, (place // 8) % 4, (place // 32) % 8, place // 256
-    dy = jnp.where(d == 7, 4, jnp.where(d % 2 == 1, -((d + 1) // 2), d // 2))
-    dx = jnp.where(xi == 3, 2, jnp.where(xi == 1, -1, xi // 2))
-    col = ((y + dy) % NY) * 16 + (zh + ab) % 2 * 8 + ((x + dx) % NX) * 2 + (c + k) % 2
-    want = col * 4 + (q + j) % 4
-    have = tile_col.reshape(SLOTS) * 4 + tile_row.reshape(SLOTS)
-    slots = jnp.arange(SLOTS, dtype=jnp.int32)
-    hit = (want[:, None] == have[None, :]) & (slots[None, :] < tile_count.reshape(1, 1))
-    return jnp.min(jnp.where(hit, slots[None, :], SLOTS), axis=1)
+def publish(*refs):
+    sources, targets, staged, sems = refs[:4], refs[4:8], refs[8:12], refs[12]
+    reads = [pltpu.make_async_copy(sources[i], staged[i], sems.at[0, i]) for i in range(4)]
+    writes = [pltpu.make_async_copy(staged[i], targets[i], sems.at[1, i]) for i in range(4)]
+    for copy in reads:
+        copy.start()
+    for read, write in zip(reads, writes):
+        read.wait()
+        write.start()
+    for copy in writes:
+        copy.wait()
 
 
 def local(
     features, node_order, tile_values, tile_row, tile_col, tile_count, weight, bias_vec, cotangent
 ):
-    table = slot_table(tile_row, tile_col, tile_count)
     vmem = pl.BlockSpec(memory_space=pltpu.VMEM)
     hbm = pl.BlockSpec(memory_space=pl.ANY)
     act, fgrad, wgrad, bgrad = pl.pallas_call(
@@ -426,9 +439,9 @@
             jax.ShapeDtypeStruct((T, 256), jnp.bfloat16),
             jax.ShapeDtypeStruct((T, T), jnp.float32),
             jax.ShapeDtypeStruct((T, 256), jnp.float32),
-            jax.ShapeDtypeStruct((8, T), jnp.float32),
+            jax.ShapeDtypeStruct((1, 256), jnp.float32),
         ),
-        in_specs=[hbm, hbm, hbm, pl.BlockSpec(memory_space=pltpu.SMEM), hbm, hbm, hbm],
+        in_specs=[hbm] * 9,
         out_specs=(vmem, vmem, vmem, vmem),
         scratch_shapes=[
             pltpu.VMEM((T, T), jnp.bfloat16),
@@ -436,6 +449,11 @@
             pltpu.VMEM((T, 256), jnp.bfloat16),
             pltpu.VMEM((1, 256), jnp.float32),
             pltpu.VMEM((T, 256), jnp.bfloat16),
+            pltpu.SMEM((1, SLOTS), jnp.int32),
+            pltpu.SMEM((1, SLOTS), jnp.int32),
+            pltpu.SMEM((1, 1), jnp.int32),
+            pltpu.VMEM((4, T), jnp.int32),
+            pltpu.SMEM((4, T), jnp.int32),
             pltpu.VMEM((SLOTS + 1, T, T), jnp.bfloat16),
             pltpu.VMEM((2, 2, ROWS, T), jnp.bfloat16),
             pltpu.VMEM((4 * T, T), jnp.float32),
@@ -449,7 +467,8 @@
             pltpu.VMEM((NY - 1, 2, 8, T), jnp.float32),
             pltpu.VMEM((NX, 8, T), jnp.float32),
             pltpu.VMEM((NZ, 4, 8, T), jnp.float32),
-            pltpu.SemaphoreType.DMA((6,)),
+            pltpu.SemaphoreType.DMA((9,)),
+            pltpu.SemaphoreType.DMA,
             pltpu.SemaphoreType.DMA((2, N_RECV)),
             pltpu.SemaphoreType.DMA((2, 6)),
             pltpu.SemaphoreType.DMA((2,)),
@@ -461,9 +480,19 @@
             collective_id=0, has_side_effects=True, vmem_limit_bytes=60 * 1024 * 1024
         ),
     )(
-        features, node_order, tile_values.reshape(SLOTS, T, T), table, weight, bias_vec.reshape(1, 256), cotangent
+        features, node_order, tile_values.reshape(SLOTS, T, T), tile_row.reshape(1, SLOTS), tile_col.reshape(1, SLOTS),
+        tile_count, weight, bias_vec.reshape(1, 256), cotangent,
     )
-    return act, fgrad, wgrad, bgrad[:2].reshape(256)
+    anywhere = pl.BlockSpec(memory_space=pl.ANY)
+    act, fgrad, wgrad, bgrad = pl.pallas_call(
+        publish,
+        out_shape=tuple(jax.ShapeDtypeStruct(a.shape, a.dtype) for a in (act, fgrad, wgrad, bgrad)),
+        in_specs=[anywhere] * 4,
+        out_specs=(anywhere,) * 4,
+        scratch_shapes=[pltpu.VMEM(a.shape, a.dtype) for a in (act, fgrad, wgrad, bgrad)] + [pltpu.SemaphoreType.DMA((2, 4))],
+        compiler_params=pltpu.CompilerParams(vmem_limit_bytes=60 * 1024 * 1024),
+    )(act, fgrad, wgrad, bgrad)
+    return act, fgrad, wgrad, bgrad.reshape(256)
 
 
 def solution(mesh):

time: 86.6 us -> 80.6 us (0.931)
  local copies, waits for them, and re-layouts: 5.75 us -> 0 us
  other arithmetic: 1.46 us -> 0 us
  Pallas kernels: 77.7 us -> 79.1 us
    unnamed x3 -> x0, local copies, waits for them, and re-layouts: 4.51 us -> none
    pallas_call x0 -> x1, Pallas kernels: none -> 1.7 us  [local(): pl.pallas_call(publish, out_shape=tuple((jax.ShapeDtypeStruct(a.shape, a....]
    reshape x1 -> x0, local copies, waits for them, and re-layouts: 1.24 us -> none  [local(): return (act, fgrad, wgrad, bgrad[:2].reshape(256))]
where the time goes in v3:
time: 80.6 us; the launch traced here: 80.4 us
  Pallas kernels  79.1 us (98%)
  between operations  1.29 us (2%)
    pallas_call x1, Pallas kernels, local(): pl.pallas_call(kernel, out_shape=(jax.ShapeDtypeStruct((T, 256), jnp.bflo...  77.4 us
    pallas_call x1, Pallas kernels, local(): pl.pallas_call(publish, out_shape=tuple((jax.ShapeDtypeStruct(a.shape, a....  1.7 us

profile of v3, /device:TPU:1, one launch (start us, length us, event | category | flops | bytes accessed | tf_op | source)
XLA Modules:
  0.0 80.4 jit_solution(15301124835021323978)
XLA Ops:
  1.3 77.4 %shard_map.120 = (bf16[128,256]{1,0:T(8,128)(2,1)}, f32[128,128]{1,0:T(8,128)}, f32[128,256]{1,0:T(8,128)}, f32[1,256]{1,0:T(1,128)}) custom-call(bf16[128,128]{1,0:T(8,128)(2,1)} %features_hbm.1, s32[1,128]{1,0:T(1,128)} %order_hbm.1, bf16[135,128,128]{2,1,0:T(8,128)(2,1)} %bitcast.5, s32[1,135]{1,0:T(1,128)} %bitcast.6, s32[1,135]{1,0:T(1,128)} %bitcast.7, ...), custom_call_target="tpu_custom_call" | custom-call | tf_op jit(solution)/shard_map/pallas_call | solution.py:436
  78.7 1.7 %shard_map.121 = (bf16[128,256]{1,0:T(8,128)(2,1)}, f32[128,128]{1,0:T(8,128)}, f32[128,256]{1,0:T(8,128)}, f32[1,256]{1,0:T(1,128)}) custom-call(bf16[128,256]{1,0:T(8,128)(2,1)} %get-tuple-element.12.refs_0_, f32[128,128]{1,0:T(8,128)} %get-tuple-element.13.refs_1_, f32[128,256]{1,0:T(8,128)} %get-tuple-element.14.refs_2_, f32[1,256]{1,0:T(1,128)} %get-tuple-element.15.refs_3_), custom_call_target="tpu_custom_call" | custom-call | tf_op jit(solution)/shard_map/pallas_call | solution.py:487

commit v4 on v3

--- a/solution.py
+++ b/solution.py
@@ -265,19 +265,36 @@
             y2(ab, 3, 5, 1, 1)
             y2(ab, 4, 6, 1, -1)
 
-        def mul(ab, d):
-            g = GROUP_OF[d]
-            ensure(sem_sib(ab, g), GROUPS[g][1] * 512)
-            base = (ab * 8 + d) * 32
-            left = jnp.concatenate([
-                jnp.concatenate([tiles[table[(base + col * 4 + j) // T, (base + col * 4 + j) % T]] for col in range(8)], axis=1) for j in range(4)
-            ], axis=0)
+        def columns(ab, d):
             pieces = []
             for xi in range(4):
                 for k in range(2):
                     pieces.append(G[p, k, pl.ds(row1(ab, d, xi), R1)])
                     pieces.append(G[p, k, pl.ds(row2(ab, xi, d), R2)])
-            acc[...] += jnp.dot(left, jnp.concatenate(pieces, axis=0), preferred_element_type=jnp.float32)
+            return pieces
+
+        def blocks(ab, d, j):
+            base = (ab * 8 + d) * 32 + j
+            return [tiles[table[(base + col * 4) // T, (base + col * 4) % T]] for col in range(8)]
+
+        def arrived(ab, d):
+            g = GROUP_OF[d]
+            ensure(sem_sib(ab, g), GROUPS[g][1] * 512)
+
+        def mul(ab, d):
+            arrived(ab, d)
+            left = jnp.concatenate([jnp.concatenate(blocks(ab, d, j), axis=1) for j in range(4)], axis=0)
+            acc[...] += jnp.dot(left, jnp.concatenate(columns(ab, d), axis=0), preferred_element_type=jnp.float32)
+
+        def last_rows(places, j):
+            total = acc[pl.ds(j * T, T)]
+            for ab, d in places:
+                arrived(ab, d)
+                total = total + jnp.dot(
+                    jnp.concatenate(blocks(ab, d, j), axis=1), jnp.concatenate(columns(ab, d), axis=0),
+                    preferred_element_type=jnp.float32,
+                )
+            return total
 
         def finish():
             for kind, n in ((SEND_Z, R1 + R2), (SEND_X1, 6 * R1), (SEND_Y1, 56 * R1), (SEND_Y2, 14 * R2), (SEND_X2, 48 * R2), (SEND_SIB, ROWS)):
@@ -294,29 +311,29 @@
             named[f"l{g}"] = functools.partial(lambda g, ab: x2_last(ab, g), g)
         for d in range(8):
             named[f"m{d}"] = functools.partial(lambda d, ab: mul(ab, d), d)
-        return named, finish
+        return named, last_rows, finish
 
     def run(p, sums, before_mul):
-        named, finish = steps(p)
-        for ab, word in PLAN:
+        named, last_rows, finish = steps(p)
+        tail = len(PLAN)
+        while PLAN[tail - 1][1][0] == "m":
+            tail -= 1
+        for ab, word in PLAN[:tail]:
             if word[0] == "m":
                 before_mul()
             if ab < 2:
                 named[word](ab)
             elif sums:
                 sums[word]()
-        return finish
-
-    def reduce_rep(p):
-        for j in range(1, 4):
-            part[p, j - 1] = acc[pl.ds(j * T, T)].astype(jnp.bfloat16)
+        places = [(ab, int(word[1])) for ab, word in PLAN[tail:]]
         for j in (3, 2, 1):
+            part[p, j - 1] = last_rows(places, j).astype(jnp.bfloat16)
             push(part.at[p, j - 1], part_in.at[p, j - 1], rs_send.at[p], rs_recv.at[p], dev_rep(j))
+        total = last_rows(places, 0)
         await_ref(part_in.at[p], rs_recv.at[p])
-        total = acc[pl.ds(0, T)]
         for j in range(3):
             total = total + part_in[p, j].astype(jnp.float32)
-        return total
+        return total, finish
 
     pending = [fill] + loads[5:]
 
@@ -324,8 +341,8 @@
         while pending:
             pending.pop().wait()
 
-    finish0 = run(0, None, loaded)
-    hidden = reduce_rep(0).astype(jnp.bfloat16)
+    total, finish0 = run(0, None, loaded)
+    hidden = total.astype(jnp.bfloat16)
     pre_act = jnp.dot(hidden, weight[...], preferred_element_type=jnp.float32) + bias[...]
     gate = jax.nn.sigmoid(pre_act)
     pre_grad = (cotangent[...].astype(jnp.float32) * gate * (1.0 + pre_act * (1.0 - gate))).astype(jnp.bfloat16)
@@ -389,8 +406,7 @@
         for j in (4, 3, 5, 2, 6, 1, 7):
             push(wfull.at[z], wfull.at[z], ar_send.at[4], ar_recv.at[4], dev_z(j))
 
-    finish1 = run(1, {"ar1": ar1, "ar2": ar2, "ar3": ar3, "ar4": ar4, "ar5": ar5}, lambda: None)
-    total = reduce_rep(1)
+    total, finish1 = run(1, {"ar1": ar1, "ar2": ar2, "ar3": ar3, "ar4": ar4, "ar5": ar5}, lambda: None)
     grad = None
     for _ in range(3):
         piece = total.astype(jnp.bfloat16)

time: 80.6 us -> 78.6 us (0.975)
  Pallas kernels: 79.1 us -> 77.2 us
    pallas_call x1, Pallas kernels: 77.4 us -> 75.5 us  [local(): pl.pallas_call(kernel, out_shape=(jax.ShapeDtypeStruct((T, 256), jnp.bflo...]
where the time goes in v4:
time: 78.6 us; the launch traced here: 78.4 us
  Pallas kernels  77.2 us (98%)
  between operations  1.29 us (2%)
    pallas_call x1, Pallas kernels, local(): pl.pallas_call(kernel, out_shape=(jax.ShapeDtypeStruct((T, 256), jnp.bflo...  75.5 us
    pallas_call x1, Pallas kernels, local(): pl.pallas_call(publish, out_shape=tuple((jax.ShapeDtypeStruct(a.shape, a....  1.7 us

profile of v4, /device:TPU:1, one launch (start us, length us, event | category | flops | bytes accessed | tf_op | source)
XLA Modules:
  0.0 78.4 jit_solution(3476373083227156075)
XLA Ops:
  1.3 75.5 %shard_map.120 = (bf16[128,256]{1,0:T(8,128)(2,1)}, f32[128,128]{1,0:T(8,128)}, f32[128,256]{1,0:T(8,128)}, f32[1,256]{1,0:T(1,128)}) custom-call(bf16[128,128]{1,0:T(8,128)(2,1)} %features_hbm.1, s32[1,128]{1,0:T(1,128)} %order_hbm.1, bf16[135,128,128]{2,1,0:T(8,128)(2,1)} %bitcast.5, s32[1,135]{1,0:T(1,128)} %bitcast.6, s32[1,135]{1,0:T(1,128)} %bitcast.7, ...), custom_call_target="tpu_custom_call" | custom-call | tf_op jit(solution)/shard_map/pallas_call | solution.py:452
  76.7 1.7 %shard_map.121 = (bf16[128,256]{1,0:T(8,128)(2,1)}, f32[128,128]{1,0:T(8,128)}, f32[128,256]{1,0:T(8,128)}, f32[1,256]{1,0:T(1,128)}) custom-call(bf16[128,256]{1,0:T(8,128)(2,1)} %get-tuple-element.12.refs_0_, f32[128,128]{1,0:T(8,128)} %get-tuple-element.13.refs_1_, f32[128,256]{1,0:T(8,128)} %get-tuple-element.14.refs_2_, f32[1,256]{1,0:T(1,128)} %get-tuple-element.15.refs_3_), custom_call_target="tpu_custom_call" | custom-call | tf_op jit(solution)/shard_map/pallas_call | solution.py:503

commit v5 on v4

--- a/solution.py
+++ b/solution.py
@@ -27,13 +27,13 @@
 
 
 PLAN = (
-    (0, "z"), (0, "y2s"), (0, "o0"), (2, "ar1"), (0, "x1s"), (0, "pl0"), (0, "y2f"), (0, "o1"), (1, "x1s"),
-    (1, "y2s"), (0, "y1n1"), (0, "y1n2"), (1, "o0"), (2, "ar2"), (0, "l0"), (0, "o2"), (0, "pl1"), (0, "pr1"),
-    (1, "y2f"), (1, "o1"), (0, "pr0"), (1, "pr0"), (1, "y1n2"), (2, "ar3"), (0, "m0"), (0, "pr2"), (0, "pl2"),
-    (1, "pl0"), (0, "y1f"), (0, "y1b"), (0, "l1"), (1, "y1n1"), (1, "o2"), (0, "m3"), (1, "pr1"), (1, "pl1"),
-    (0, "m1"), (0, "m4"), (1, "y1f"), (1, "l0"), (0, "l2"), (0, "m2"), (0, "y1l"), (2, "ar4"), (1, "pr2"), (1, "y1b"),
-    (1, "pl2"), (1, "m0"), (1, "l1"), (0, "m7"), (0, "m5"), (0, "m6"), (1, "m1"), (1, "y1l"), (1, "m2"), (1, "l2"),
-    (2, "ar5"), (1, "m3"), (1, "m4"), (1, "m6"), (1, "m7"), (1, "m5"),
+    (0, "z"), (0, "y2s"), (0, "x1s"), (2, "ar1"), (0, "y1n1"), (0, "o0"), (0, "y2f"), (0, "o1"), (1, "x1s"),
+    (1, "y2s"), (0, "pl0"), (1, "o0"), (0, "pr0"), (0, "y1n2"), (2, "ar2"), (0, "o2"), (0, "pl1"), (0, "pr1"),
+    (1, "y2f"), (1, "pr0"), (1, "o1"), (1, "y1n2"), (0, "l0"), (2, "ar3"), (0, "m0"), (0, "y1f"), (0, "pr2"),
+    (1, "pl0"), (1, "y1n1"), (0, "pl2"), (0, "y1b"), (0, "l1"), (1, "o2"), (1, "l0"), (0, "m2"), (0, "m3"),
+    (1, "pl1"), (1, "pr1"), (1, "y1f"), (0, "m4"), (1, "m0"), (0, "l2"), (0, "y1l"), (2, "ar4"), (1, "pr2"),
+    (0, "m1"), (1, "pl2"), (1, "y1b"), (0, "m7"), (1, "l1"), (0, "m5"), (0, "m6"), (1, "y1l"), (1, "m2"), (1, "m3"),
+    (1, "l2"), (2, "ar5"), (1, "m4"), (1, "m1"), (1, "m5"), (1, "m6"), (1, "m7"),
 )
 
 

time: 78.6 us -> 78.5 us (level)
  no operation moved by 1% of the time
where the time goes in v5:
time: 78.5 us; the launch traced here: 78.3 us
  Pallas kernels  77.1 us (98%)
  between operations  1.29 us (2%)
    pallas_call x1, Pallas kernels, local(): pl.pallas_call(kernel, out_shape=(jax.ShapeDtypeStruct((T, 256), jnp.bflo...  75.4 us
    pallas_call x1, Pallas kernels, local(): pl.pallas_call(publish, out_shape=tuple((jax.ShapeDtypeStruct(a.shape, a....  1.7 us

profile of v5, /device:TPU:1, one launch (start us, length us, event | category | flops | bytes accessed | tf_op | source)
XLA Modules:
  0.0 78.3 jit_solution(5150468313519434724)
XLA Ops:
  1.3 75.4 %shard_map.120 = (bf16[128,256]{1,0:T(8,128)(2,1)}, f32[128,128]{1,0:T(8,128)}, f32[128,256]{1,0:T(8,128)}, f32[1,256]{1,0:T(1,128)}) custom-call(bf16[128,128]{1,0:T(8,128)(2,1)} %features_hbm.1, s32[1,128]{1,0:T(1,128)} %order_hbm.1, bf16[135,128,128]{2,1,0:T(8,128)(2,1)} %bitcast.5, s32[1,135]{1,0:T(1,128)} %bitcast.6, s32[1,135]{1,0:T(1,128)} %bitcast.7, ...), custom_call_target="tpu_custom_call" | custom-call | tf_op jit(solution)/shard_map/pallas_call | solution.py:452
  76.6 1.7 %shard_map.121 = (bf16[128,256]{1,0:T(8,128)(2,1)}, f32[128,128]{1,0:T(8,128)}, f32[128,256]{1,0:T(8,128)}, f32[1,256]{1,0:T(1,128)}) custom-call(bf16[128,256]{1,0:T(8,128)(2,1)} %get-tuple-element.12.refs_0_, f32[128,128]{1,0:T(8,128)} %get-tuple-element.13.refs_1_, f32[128,256]{1,0:T(8,128)} %get-tuple-element.14.refs_2_, f32[1,256]{1,0:T(1,128)} %get-tuple-element.15.refs_3_), custom_call_target="tpu_custom_call" | custom-call | tf_op jit(solution)/shard_map/pallas_call | solution.py:503
